TPU v7x, 128 devices: a whole 4x4x4 slice. The times are simulated.
128 devices in a mesh: dp: 32 (over y, x, core), tensor: 4 (over z).
Axes of the slice: x: 4, y: 4, z: 4, core: 2. Of those that a mesh axis runs over, the one named last changes fastest.
Arguments:
- activations: bfloat16 [32768, 3584], P('dp'), may hold values from -60 to 60
- out_grads: bfloat16 [32768, 3584], P('dp', 'tensor'), may hold values from -6 to 6
- error_buffer: bfloat16 [32, 3584, 3584], P('dp', None, 'tensor'), may hold values from -6 to 6
- basis_q: float32 [3584, 32], P('tensor'), may hold values from -6 to 6
Outputs:
- update: bfloat16 [3584, 3584], P(None, 'tensor')
- new_error: bfloat16 [32, 3584, 3584], P('dp', None, 'tensor')
- next_q: float32 [3584, 32], P('tensor')
All inputs are finite; a program needn't handle non-finite values.
Results may differ from a plain program's by a relative error of at most 0.001.
Values sent between devices are 32-bit elements; how exact they have to be, the bound alone decides.
A program may use at most 128 MiB of HBM per device.

v0:
```python
import jax
import jax.numpy as jnp
from jax import lax
from jax.sharding import PartitionSpec as P


def orthonormal(p_sum, gram):
    factor = jnp.linalg.cholesky(gram)
    return lax.linalg.triangular_solve(factor, p_sum, left_side=False, lower=True, transpose_a=True)


def shards(activations, out_grads, error_buffer, basis_q):
    tok_rows = activations.shape[0]
    grad = lax.dot_general(
        activations, out_grads, (((0,), (0,)), ((), ())), preferred_element_type=jnp.float32
    )
    corrected = grad / jnp.sqrt(jnp.float32(tok_rows)) + error_buffer[0].astype(jnp.float32)
    p_term = jnp.dot(corrected, basis_q, precision=lax.Precision.HIGHEST)
    p_sum = lax.psum(p_term, ("dp", "tensor"))
    gram = jnp.dot(p_sum.T, p_sum, precision=lax.Precision.HIGHEST)
    p_hat = orthonormal(p_sum, gram)
    q_local = jnp.dot(corrected.T, p_hat, precision=lax.Precision.HIGHEST)
    q_sum = lax.psum(q_local, "dp")
    next_q = q_sum / jnp.float32(lax.axis_size("dp"))
    update = jnp.dot(p_hat, next_q.T, precision=lax.Precision.HIGHEST).astype(jnp.bfloat16)
    fresh = corrected - jnp.dot(p_hat, q_local.T, precision=lax.Precision.HIGHEST)
    new_error = fresh.astype(jnp.bfloat16)[None]
    return (update, new_error, next_q)


def solution(mesh):
    in_specs = (P("dp", None), P("dp", "tensor"), P("dp", None, "tensor"), P("tensor", None))
    out_specs = (P(None, "tensor"), P("dp", None, "tensor"), P("tensor", None))
    return jax.shard_map(shards, mesh=mesh, in_specs=in_specs, out_specs=out_specs, check_vma=False)
```

profile of v0, /device:TPU:1, one launch (start us, length us, event | category | flops | bytes accessed | tf_op | source)
XLA Modules:
  0.0 340.7 jit_solution(15980669766137202224)
XLA Ops:
  7.2 0.0 copy-start
  7.2 0.0 copy-start.4
  7.2 0.0 all-reduce.3.cloned.1.call-start
  7.2 1.4 copy-done
  8.7 11.3 %convert_add_fusion = f32[3584,896]{1,0:T(8,128)S(1)} fusion(bf16[1024,3584]{1,0:T(8,128)(2,1)} %param.4, bf16[1024,896]{1,0:T(8,128)(2,1)S(1)} %copy-done, bf16[1,3584,896]{2,1,0:T(8,128)(2,1)} %param.6), kind=kOutput, calls=%fused_computation | convolution fusion | flops 6586302464 | bytes 28442624 | tf_op jit(solution)/shard_map/dot_general | solution.py:14
  20.0 0.0 copy-start.1
  20.0 4.6 %copy-done.1 = f32[3584,896]{1,0:T(8,128)} copy-done((f32[3584,896]{1,0:T(8,128)}, f32[3584,896]{1,0:T(8,128)S(1)}, u32[]{:S(2)}) %copy-start.1) | copy-done | bytes 12845080
  24.6 0.0 copy-done.4
  24.6 12.7 %fusion.5 = f32[3584,32]{0,1:T(8,128)} fusion(f32[3584,896]{1,0:T(8,128)S(1)} %convert_add_fusion, f32[896,32]{0,1:T(8,128)S(1)} %copy-done.4), kind=kOutput, calls=%fused_computation.15 | convolution fusion | flops 1233125376 | bytes 13418496 | tf_op jit(solution)/shard_map/dot_general | solution.py:18
  37.3 0.0 all-reduce.3.cloned.1.call-update
  37.3 147.7 %all-reduce.3.cloned.1.call-done = f32[3584,32]{0,1:T(8,128)} async-done(((f32[3584,32]{0,1:T(8,128)}), f32[3584,32]{0,1:T(8,128)}) %all-reduce.3.cloned.1.call-update) | async-done | bytes 458768 | tf_op jit(solution)/shard_map/psum | solution.py:19
  185.0 1.7 fusion.6
  186.7 0.1 copy.7
  186.8 2.9 cholesky.16
  189.7 0.6 compare_reduce_fusion
  190.4 0.7 fusion.1
  191.0 2.4 custom-call.6
  193.5 1.6 fusion.2
  195.1 10.3 %fusion.7 = f32[896,32]{0,1:T(8,128)S(1)} fusion(f32[3584,896]{1,0:T(8,128)} %copy-done.1, f32[3584,32]{0,1:T(8,128)S(1)} %fusion.2), kind=kOutput, calls=%fused_computation.17 | convolution fusion | flops 1233125376 | bytes 13418496 | tf_op jit(solution)/shard_map/dot_general | solution.py:22
  205.4 0.0 copy-start.2
  205.4 14.1 %fusion = bf16[1,3584,896]{2,1,0:T(8,128)(2,1)} fusion(f32[3584,896]{1,0:T(8,128)} %copy-done.1, f32[3584,32]{0,1:T(8,128)S(1)} %fusion.2, f32[896,32]{0,1:T(8,128)S(1)} %fusion.7), kind=kOutput, calls=%fused_computation.3 | convolution fusion | flops 1239547904 | bytes 19841024 | tf_op jit(solution)/shard_map/dot_general | solution.py:26
  219.5 0.0 all-reduce.5.cloned.1.call-start
  219.5 0.0 copy-done.2
  219.5 0.7 all-reduce.5.cloned.1.call-update
  220.2 100.7 %all-reduce.5.cloned.1.call-done = f32[896,32]{0,1:T(8,128)} async-done(((f32[896,32]{0,1:T(8,128)}), f32[896,32]{0,1:T(8,128)}) %all-reduce.5.cloned.1.call-update) | async-done | bytes 114704 | tf_op jit(solution)/shard_map/psum | solution.py:23
  320.9 0.9 broadcast_multiply_fusion
  321.8 0.0 copy-start.3
  321.8 12.1 %convolution_convert_fusion = bf16[3584,896]{1,0:T(8,128)(2,1)} fusion(f32[3584,32]{0,1:T(8,128)S(1)} %fusion.2, f32[896,32]{0,1:T(8,128)S(1)} %broadcast_multiply_fusion), kind=kOutput, calls=%fused_computation.2 | convolution fusion | flops 1236336640 | bytes 6995968 | tf_op jit(solution)/shard_map/dot_general | solution.py:25
  333.9 0.0 copy-done.3
  (2 shorter events, 0.0 us)
Async XLA Ops:
  7.2 1.5 copy-start
  7.2 17.4 %copy-start.4 = (f32[896,32]{0,1:T(8,128)S(1)}, f32[896,32]{0,1:T(8,128)}, u32[]{:S(2)}) copy-start(f32[896,32]{0,1:T(8,128)} %param.7) | copy-start | bytes 344068
  7.2 177.8 %all-reduce.3.cloned.1.call-start = ((), (), s32[]{:S(2)}) async-start(), calls=%async_computation | async-start | bytes 917504 | tf_op jit(solution)/shard_map/psum | solution.py:19
  20.0 4.6 %copy-start.1 = (f32[3584,896]{1,0:T(8,128)}, f32[3584,896]{1,0:T(8,128)S(1)}, u32[]{:S(2)}) copy-start(f32[3584,896]{1,0:T(8,128)S(1)} %convert_add_fusion) | copy-start | bytes 38535172
  205.4 14.1 %copy-start.2 = (f32[896,32]{0,1:T(8,128)}, f32[896,32]{0,1:T(8,128)S(1)}, u32[]{:S(2)}) copy-start(f32[896,32]{0,1:T(8,128)S(1)} %fusion.7) | copy-start | bytes 344068
  219.5 101.4 %all-reduce.5.cloned.1.call-start = ((), (), s32[]{:S(2)}) async-start(), calls=%async_computation.1 | async-start | bytes 229376 | tf_op jit(solution)/shard_map/psum | solution.py:23
  321.8 12.1 %copy-start.3 = (f32[896,32]{0,1:T(8,128)}, f32[896,32]{0,1:T(8,128)S(1)}, u32[]{:S(2)}) copy-start(f32[896,32]{0,1:T(8,128)S(1)} %broadcast_multiply_fusion) | copy-start | bytes 344068
Sparse Core Ops, SparseCore 0:
  37.5 147.5 all-reduce.2
  224.5 96.3 all-reduce.4
where the time goes:
time: 341 us
  waiting for transfers between devices  249 us (73%)
  matrix products  63.7 us (19%)
  between operations  14.1 us (4%)
  other arithmetic  7.6 us (2%)
  local copies, waits for them, and re-layouts  6.13 us (2%)
    psum x1, waiting for transfers between devices, shards(): p_sum = lax.psum(p_term, ('dp', 'tensor'))  148 us
    psum x1, waiting for transfers between devices, shards(): q_sum = lax.psum(q_local, 'dp')  101 us
    dot_general x1, matrix products, shards(): jnp.dot(p_hat, q_local.T, precision=lax.Precision.HIGHEST)  14.1 us
    dot_general x1, matrix products, shards(): p_term = jnp.dot(corrected, basis_q, precision=lax.Precision.HIGHEST)  12.7 us
    dot_general x1, matrix products, shards(): jnp.dot(p_hat, next_q.T, precision=lax.Precision.HIGHEST)  12.1 us
    dot_general x1, matrix products, shards(): lax.dot_general(activations, out_grads, (((0,), (0,)), ((), ())), preferr...  11.3 us
    dot_general x1, matrix products, shards(): q_local = jnp.dot(corrected.T, p_hat, precision=lax.Precision.HIGHEST)  10.3 us
  transfers between devices with their start and end apart: 2, of which 2 were waited for; matrix products, arithmetic and copies ran while one was open for 0% of the time, Pallas kernels for 0%

commit v1 on v0

v1 whole, which is shorter than its diff:
```python
import jax
import jax.numpy as jnp
from jax import lax
from jax.experimental import pallas as pl
from jax.experimental.pallas import tpu as pltpu
from jax.sharding import PartitionSpec as P

MESH = pl.DeviceIdType.MESH
F32 = jnp.float32
BF16 = jnp.bfloat16

ROWS = 3584
COLS = 896
TOK = 1024
RANK = 32
HALF = RANK // 2
CHUNK = 512
N_CHUNK = ROWS // CHUNK
CHIPS = 64
DPS = 32
LANES = 128
P_TILES = 56
Q_TILES = 28
SCALE = 1.0 / 32.0

NN = (((1,), (0,)), ((), ()))
NT = (((1,), (1,)), ((), ()))
TN = (((0,), (0,)), ((), ()))


def mm(a, b, dims=NN):
    return lax.dot_general(a, b, dims, preferred_element_type=F32)


def split2(x):
    hi = x.astype(BF16)
    lo = (x - hi.astype(F32)).astype(BF16)
    return hi, lo


def split3(x):
    hi = x.astype(BF16)
    rest = x - hi.astype(F32)
    mid = rest.astype(BF16)
    lo = (rest - mid.astype(F32)).astype(BF16)
    return hi, mid, lo


def fold3(x):
    return x[:RANK] + x[RANK:2 * RANK] + x[2 * RANK:]


def inverse_factor(gram):
    row_id = lax.broadcasted_iota(jnp.int32, (RANK, LANES), 0)
    lane_id = lax.broadcasted_iota(jnp.int32, (RANK, LANES), 1)
    eye = (lane_id == row_id + RANK).astype(F32)
    work = jnp.concatenate([gram, jnp.zeros((RANK, LANES - RANK), F32)], axis=1) + eye
    scale = jnp.zeros((RANK, LANES), F32)
    for j in range(RANK):
        row = work[j:j + 1, :]
        piv = jnp.broadcast_to(work[j:j + 1, j:j + 1], (1, LANES))
        col = jnp.broadcast_to(work[:, j:j + 1], (RANK, LANES))
        scale = jnp.where(row_id == j, piv, scale)
        work = work - jnp.where(row_id > j, col * (row / piv), 0.0)
    return (work * lax.rsqrt(scale))[:, RANK:2 * RANK]


def body(a_hbm, g_hbm, e_hbm, q_ref, c_ref, phat_ref, qloc_ref, nextq_ref,
         a_buf, g_buf, e_buf, qs, gqs, p_loc, core_buf, p_sum, p_full, p_recv, psplit,
         q_raw, q_recv, q_full,
         a_sem, g_sem, e_sem, cs_sem, cr_sem, rs_send, rs_recv, ag_send, ag_recv,
         x_send, x_recv, qs_send, qs_recv, qa_send, qa_recv):
    dp = lax.axis_index("dp")
    z = lax.axis_index("tensor")
    core = dp % 2
    plane = dp // 2
    chip = plane * 4 + z
    sib = (plane * 2 + 1 - core, z)

    def chip_dev(k):
        return ((k // 4) * 2 + core, k % 4)

    g_copy = pltpu.make_async_copy(g_hbm, g_buf, g_sem)
    g_copy.start()
    a_copies = []
    e_copies = []
    for j in range(N_CHUNK):
        cols = pl.ds(j * CHUNK, CHUNK)
        a_copies.append(pltpu.make_async_copy(a_hbm.at[:, cols], a_buf.at[j], a_sem.at[j]))
        e_copies.append(pltpu.make_async_copy(e_hbm.at[cols, :], e_buf.at[cols, :], e_sem.at[j]))
        a_copies[j].start()
        e_copies[j].start()

    bar = pltpu.get_barrier_semaphore()
    pl.semaphore_signal(bar, inc=1, device_id=sib, device_id_type=MESH)

    @pl.loop(0, CHIPS)
    def _(k):
        @pl.when(k != chip)
        def _():
            pl.semaphore_signal(bar, inc=1, device_id=chip_dev(k), device_id_type=MESH)

    @pl.loop(0, DPS)
    def _(k):
        @pl.when(k % 2 != core)
        def _():
            @pl.when(k // 2 != plane)
            def _():
                pl.semaphore_signal(bar, inc=1, device_id=(k, z), device_id_type=MESH)

    for i, part in enumerate(split3(q_ref[...])):
        qs[i * RANK:(i + 1) * RANK, :] = part
    g_copy.wait()
    gq = fold3(mm(qs[...], g_buf[...], NT)) * SCALE
    for i, part in enumerate(split3(gq)):
        gqs[i * RANK:(i + 1) * RANK, :] = part

    mine = pl.multiple_of(core * HALF, HALF)
    other = pl.multiple_of(HALF - core * HALF, HALF)

    def core_copy(j):
        cols = pl.ds(j * CHUNK, CHUNK)
        return pltpu.make_async_remote_copy(
            src_ref=p_loc.at[pl.ds(other, HALF), cols], dst_ref=core_buf.at[:, cols],
            send_sem=cs_sem.at[j], recv_sem=cr_sem.at[j], device_id=sib, device_id_type=MESH)

    def scatter(j):
        cols = pl.ds(j * CHUNK, CHUNK)
        core_copy(j).wait_recv()
        p_sum[:, cols] = p_loc[pl.ds(mine, HALF), cols] + core_buf[:, cols]

        def send(i, carry):
            owner = i * 8 + j
            rows = pl.ds(pl.multiple_of((i // 4) * 8, 8), 8)
            lanes = pl.ds(pl.multiple_of(j * CHUNK + (i % 4) * LANES, LANES), LANES)

            @pl.when(owner != chip)
            def _():
                pltpu.make_async_remote_copy(
                    src_ref=p_sum.at[rows, lanes], dst_ref=p_recv.at[chip],
                    send_sem=rs_send, recv_sem=rs_recv,
                    device_id=chip_dev(owner), device_id_type=MESH).start()

            @pl.when(owner == chip)
            def _():
                p_recv[chip] = p_sum[rows, lanes]
            return carry
        lax.fori_loop(0, 8, send, 0)

    for j in range(N_CHUNK):
        cols = pl.ds(j * CHUNK, CHUNK)
        a_copies[j].wait()
        e_copies[j].wait()
        p_loc[:, cols] = fold3(mm(gqs[...], a_buf[j]) + mm(qs[...], e_buf[cols, :], NT))
        if j == 0:
            pl.semaphore_wait(bar, 1 + (CHIPS - 1) + (DPS // 2 - 1))
        core_copy(j).start()
        if j > 0:
            scatter(j - 1)

    def correct(j):
        cols = pl.ds(j * CHUNK, CHUNK)
        c_ref[cols, :] = mm(a_buf[j], g_buf[...], TN) * SCALE + e_buf[cols, :].astype(F32)

    correct(0)
    scatter(N_CHUNK - 1)
    for j in range(1, N_CHUNK):
        correct(j)

    t_i = chip // 8
    t_j = chip % 8
    owns = t_j < N_CHUNK
    t_rows = pl.ds(pl.multiple_of(core * HALF + (t_i // 4) * 8, 8), 8)
    t_lanes = pl.ds(pl.multiple_of(jnp.minimum(t_j, N_CHUNK - 1) * CHUNK + (t_i % 4) * LANES, LANES), LANES)

    @pl.when(owns)
    def _():
        got = p_recv.at[pl.ds(0, CHIPS - 1)]
        pltpu.make_async_copy(got, got, rs_recv).wait()
        p_full[t_rows, t_lanes] = jnp.sum(p_recv[...], axis=0)

        def send(k, carry):
            @pl.when(k != chip)
            def _():
                pltpu.make_async_remote_copy(
                    src_ref=p_full.at[t_rows, t_lanes], dst_ref=p_full.at[t_rows, t_lanes],
                    send_sem=ag_send, recv_sem=ag_recv,
                    device_id=chip_dev(k), device_id_type=MESH).start()
            return carry
        lax.fori_loop(0, CHIPS, send, 0)
        most = p_recv.at[pl.ds(0, P_TILES - 1)]
        pltpu.make_async_copy(most, most, ag_recv).wait()

    @pl.when(jnp.logical_not(owns))
    def _():
        most = p_recv.at[pl.ds(0, P_TILES)]
        pltpu.make_async_copy(most, most, ag_recv).wait()

    half = p_full.at[pl.ds(mine, HALF), :]
    swap = pltpu.make_async_remote_copy(
        src_ref=half, dst_ref=half, send_sem=x_send, recv_sem=x_recv,
        device_id=sib, device_id_type=MESH)
    swap.start()
    swap.wait()

    for i, part in enumerate(split3(p_full[...])):
        psplit[i * RANK:(i + 1) * RANK, :] = part
    acc = jnp.zeros((RANK, COLS), F32)
    for j in range(N_CHUNK):
        cols = pl.ds(j * CHUNK, CHUNK)
        hi, lo = split2(c_ref[cols, :])
        acc = acc + fold3(mm(psplit[:, cols], hi) + mm(psplit[:, cols], lo))
    q_raw[...] = acc

    def q_send(t, carry):
        rows = pl.ds(pl.multiple_of((t // 7) * 8, 8), 8)
        lanes = pl.ds(pl.multiple_of((t % 7) * LANES, LANES), LANES)

        @pl.when(t != dp)
        def _():
            pltpu.make_async_remote_copy(
                src_ref=q_raw.at[rows, lanes], dst_ref=q_recv.at[dp],
                send_sem=qs_send, recv_sem=qs_recv, device_id=(t, z), device_id_type=MESH).start()

        @pl.when(t == dp)
        def _():
            q_recv[dp] = q_raw[rows, lanes]
        return carry
    lax.fori_loop(0, Q_TILES, q_send, 0)

    gram9 = mm(psplit[...], psplit[...], NT)
    gram = jnp.zeros((RANK, RANK), F32)
    for r in range(3):
        for c in range(3):
            gram = gram + gram9[r * RANK:(r + 1) * RANK, c * RANK:(c + 1) * RANK]
    inv = inverse_factor(gram)

    q_owns = dp < Q_TILES
    t = jnp.minimum(dp, Q_TILES - 1)
    q_rows = pl.ds(pl.multiple_of((t // 7) * 8, 8), 8)
    q_lanes = pl.ds(pl.multiple_of((t % 7) * LANES, LANES), LANES)

    @pl.when(q_owns)
    def _():
        got = q_recv.at[pl.ds(0, DPS - 1)]
        pltpu.make_async_copy(got, got, qs_recv).wait()
        q_full[q_rows, q_lanes] = jnp.sum(q_recv[...], axis=0)

        def send(k, carry):
            @pl.when(k != dp)
            def _():
                pltpu.make_async_remote_copy(
                    src_ref=q_full.at[q_rows, q_lanes], dst_ref=q_full.at[q_rows, q_lanes],
                    send_sem=qa_send, recv_sem=qa_recv, device_id=(k, z), device_id_type=MESH).start()
            return carry
        lax.fori_loop(0, DPS, send, 0)

    inv_parts = split3(inv)
    inv_left = jnp.concatenate([inv_parts[0], inv_parts[0], inv_parts[1], inv_parts[0], inv_parts[1], inv_parts[2]], axis=1)

    def six(parts):
        return jnp.concatenate([parts[0], parts[1], parts[0], parts[2], parts[1], parts[0]], axis=0)

    p_hat = mm(inv_left, six((psplit[:RANK, :], psplit[RANK:2 * RANK, :], psplit[2 * RANK:, :])))
    ph = jnp.transpose(p_hat)
    ph_hi, ph_lo = split2(ph)
    phat_ref[:, :RANK] = ph_hi
    phat_ref[:, RANK:2 * RANK] = ph_hi
    phat_ref[:, 2 * RANK:] = ph_lo
    q_hi, q_lo = split2(mm(inv_left, six(split3(q_raw[...]))))
    qloc_ref[:RANK, :] = q_hi
    qloc_ref[RANK:2 * RANK, :] = q_lo
    qloc_ref[2 * RANK:, :] = q_hi

    @pl.when(q_owns)
    def _():
        most = q_recv.at[pl.ds(0, Q_TILES - 1)]
        pltpu.make_async_copy(most, most, qa_recv).wait()

    @pl.when(jnp.logical_not(q_owns))
    def _():
        most = q_recv.at[pl.ds(0, Q_TILES)]
        pltpu.make_async_copy(most, most, qa_recv).wait()

    nextq_ref[...] = mm(inv_left, six(split3(q_full[...]))) * (1.0 / DPS)

    for j in range(N_CHUNK):
        core_copy(j).wait_send()

    @pl.when(owns)
    def _():
        sent = p_recv.at[pl.ds(0, P_TILES - 1)]
        pltpu.make_async_copy(sent, sent, rs_send).wait()
        sent = p_recv.at[pl.ds(0, CHIPS - 1)]
        pltpu.make_async_copy(sent, sent, ag_send).wait()

    @pl.when(jnp.logical_not(owns))
    def _():
        sent = p_recv.at[pl.ds(0, P_TILES)]
        pltpu.make_async_copy(sent, sent, rs_send).wait()

    @pl.when(q_owns)
    def _():
        sent = q_recv.at[pl.ds(0, Q_TILES - 1)]
        pltpu.make_async_copy(sent, sent, qs_send).wait()
        sent = q_recv.at[pl.ds(0, DPS - 1)]
        pltpu.make_async_copy(sent, sent, qa_send).wait()

    @pl.when(jnp.logical_not(q_owns))
    def _():
        sent = q_recv.at[pl.ds(0, Q_TILES)]
        pltpu.make_async_copy(sent, sent, qs_send).wait()


def factors(a, g, e, q):
    vm = pl.BlockSpec(memory_space=pltpu.VMEM)
    hbm = pl.BlockSpec(memory_space=pltpu.HBM)
    dma = pltpu.SemaphoreType.DMA
    return pl.pallas_call(
        body,
        out_shape=(
            pltpu.VMEM((ROWS, COLS), F32),
            pltpu.VMEM((ROWS, 3 * RANK), BF16),
            pltpu.VMEM((3 * RANK, COLS), BF16),
            pltpu.VMEM((RANK, COLS), F32),
        ),
        in_specs=[hbm, hbm, hbm, vm],
        out_specs=(vm, vm, vm, vm),
        scratch_shapes=[
            pltpu.VMEM((N_CHUNK, TOK, CHUNK), BF16),
            pltpu.VMEM((TOK, COLS), BF16),
            pltpu.VMEM((ROWS, COLS), BF16),
            pltpu.VMEM((3 * RANK, COLS), BF16),
            pltpu.VMEM((3 * RANK, TOK), BF16),
            pltpu.VMEM((RANK, ROWS), F32),
            pltpu.VMEM((HALF, ROWS), F32),
            pltpu.VMEM((HALF, ROWS), F32),
            pltpu.VMEM((RANK, ROWS), F32),
            pltpu.VMEM((CHIPS, 8, LANES), F32),
            pltpu.VMEM((3 * RANK, ROWS), BF16),
            pltpu.VMEM((RANK, COLS), F32),
            pltpu.VMEM((DPS, 8, LANES), F32),
            pltpu.VMEM((RANK, COLS), F32),
            dma((N_CHUNK,)), dma, dma((N_CHUNK,)), dma((N_CHUNK,)), dma((N_CHUNK,)),
            dma, dma, dma, dma, dma, dma, dma, dma, dma, dma,
        ],
        compiler_params=pltpu.CompilerParams(
            collective_id=0, has_side_effects=True, vmem_limit_bytes=36 * 2**20),
        name="factors",
    )(a, g, e, q)


def out_body(c_ref, phat_ref, qloc_ref, nextq_ref, upd_ref, err_ref, nq_ref, nqs):
    @pl.when(pl.program_id(0) == 0)
    def _():
        hi, lo = split2(nextq_ref[...])
        nqs[:RANK, :] = hi
        nqs[RANK:2 * RANK, :] = lo
        nqs[2 * RANK:, :] = hi
        nq_ref[...] = nextq_ref[...]
    rows = pl.ds(pl.multiple_of(pl.program_id(0) * CHUNK, CHUNK), CHUNK)
    ph = phat_ref[rows, :]
    err_ref[...] = (c_ref[rows, :] - mm(ph, qloc_ref[...])).astype(BF16)
    upd_ref[...] = mm(ph, nqs[...]).astype(BF16)


def outputs(c, phat, qloc, nextq):
    vm = pl.BlockSpec(memory_space=pltpu.VMEM)
    block = pl.BlockSpec((CHUNK, COLS), lambda i: (i, 0))
    return pl.pallas_call(
        out_body,
        grid=(N_CHUNK,),
        out_shape=(
            jax.ShapeDtypeStruct((ROWS, COLS), BF16),
            jax.ShapeDtypeStruct((ROWS, COLS), BF16),
            jax.ShapeDtypeStruct((RANK, COLS), F32),
        ),
        in_specs=[vm, vm, vm, vm],
        out_specs=(block, block, pl.BlockSpec((RANK, COLS), lambda i: (0, 0))),
        scratch_shapes=[pltpu.VMEM((3 * RANK, COLS), BF16)],
        compiler_params=pltpu.CompilerParams(vmem_limit_bytes=24 * 2**20),
        name="outputs",
    )(c, phat, qloc, nextq)


def shards(activations, out_grads, error_buffer, basis_q):
    c, phat, qloc, nextq = factors(activations, out_grads, error_buffer[0], basis_q.T)
    update, new_error, next_q = outputs(c, phat, qloc, nextq)
    return update, new_error[None], next_q.T


def solution(mesh):
    in_specs = (P("dp", None), P("dp", "tensor"), P("dp", None, "tensor"), P("tensor", None))
    out_specs = (P(None, "tensor"), P("dp", None, "tensor"), P("tensor", None))
    return jax.shard_map(shards, mesh=mesh, in_specs=in_specs, out_specs=out_specs, check_vma=False)
```

time: 341 us -> 55.1 us (0.16)
  waiting for transfers between devices: 249 us -> 0 us
  matrix products: 63.7 us -> 0 us
  Pallas kernels: 0 us -> 51.9 us
  between operations: 14.1 us -> 0.65 us
  other arithmetic: 7.6 us -> 0 us
  local copies, waits for them, and re-layouts: 6.13 us -> 2.39 us
    psum x2 -> x0, waiting for transfers between devices: 248 us -> none  [the longest x1 148 us: shards(): p_sum = lax.psum(p_term, ('dp', 'tensor'))]
    dot_general x6 -> x0, matrix products: 62.1 us -> none  [the longest x1 14.1 us: shards(): jnp.dot(p_hat, q_local.T, precision=lax.Precision.HIGHEST)]
    pallas_call x0 -> x2, Pallas kernels: none -> 51.9 us  [the longest x1 45 us: factors(): pl.pallas_call(body, out_shape=(pltpu.VMEM((ROWS, COLS), F32), pltpu.VMEM...]
    another operation x5 -> x0, other arithmetic: 6.68 us -> none  [the longest x3 3.6 us: orthonormal(): factor = jnp.linalg.cholesky(gram)]
    unnamed x10 -> x4, local copies, waits for them, and re-layouts: 6.06 us -> 2.39 us
  transfers between devices with their start and end apart: 2 -> 0, of which waited for: 2 -> 0; matrix products, arithmetic and copies ran while one was open for 0% -> 0% of each run, Pallas kernels for 0% -> 0%
where the time goes in v1:
time: 55.1 us; the launch traced here: 54.9 us
  Pallas kernels  51.9 us (94%)
  local copies, waits for them, and re-layouts  2.39 us (4%)
  between operations  0.65 us (1%)
    pallas_call x1, Pallas kernels, factors(): pl.pallas_call(body, out_shape=(pltpu.VMEM((ROWS, COLS), F32), pltpu.VMEM...  45 us
    pallas_call x1, Pallas kernels, outputs(): pl.pallas_call(out_body, grid=(N_CHUNK,), out_shape=(jax.ShapeDtypeStruct...  6.91 us
    unnamed x4, local copies, waits for them, and re-layouts  2.39 us

profile of v1, /device:TPU:1, one launch (start us, length us, event | category | flops | bytes accessed | tf_op | source)
XLA Modules:
  0.0 54.9 jit_solution(14204491911557371946)
XLA Ops:
  0.6 0.0 copy-start
  0.6 1.5 %copy-done = bf16[1024,896]{1,0:T(8,128)(2,1)S(1)} copy-done((bf16[1024,896]{1,0:T(8,128)(2,1)S(1)}, bf16[1024,896]{1,0:T(8,128)(2,1)}, u32[]{:S(2)}) %copy-start) | copy-done | bytes 1835032
  2.1 0.0 copy-start.1
  2.1 0.9 %copy-done.1 = f32[896,32]{0,1:T(8,128)S(1)} copy-done((f32[896,32]{0,1:T(8,128)S(1)}, f32[896,32]{0,1:T(8,128)}, u32[]{:S(2)}) %copy-start.1) | copy-done | bytes 114712
  3.0 45.0 %factors.1 = (f32[3584,896]{1,0:T(8,128)S(1)}, bf16[3584,96]{1,0:T(8,128)(2,1)S(1)}, bf16[96,896]{1,0:T(8,128)(2,1)S(1)}, f32[32,896]{1,0:T(8,128)S(1)}) custom-call(bf16[1024,3584]{1,0:T(8,128)(2,1)} %a_hbm.1, bf16[1024,896]{1,0:T(8,128)(2,1)S(1)} %copy-done, bf16[3584,896]{1,0:T(8,128)(2,1)} %bitcast.5, f32[32,896]{1,0:T(8,128)S(1)} %bitcast.4), custom_call_target="tpu_custom_call" | custom-call | tf_op jit(solution)/shard_map/factors/pallas_call | solution.py:319
  48.0 6.9 %outputs.1 = (bf16[3584,896]{1,0:T(8,128)(2,1)}, bf16[3584,896]{1,0:T(8,128)(2,1)}, f32[32,896]{1,0:T(8,128)}) custom-call(f32[3584,896]{1,0:T(8,128)S(1)} %get-tuple-element.10.c_ref, bf16[3584,96]{1,0:T(8,128)(2,1)S(1)} %get-tuple-element.11.phat_ref, bf16[96,896]{1,0:T(8,128)(2,1)S(1)} %get-tuple-element.12.qloc_ref, ...), custom_call_target="tpu_custom_call" | custom-call | tf_op jit(solution)/shard_map/outputs/pallas_call | solution.py:370
Async XLA Ops:
  0.6 1.5 %copy-start = (bf16[1024,896]{1,0:T(8,128)(2,1)S(1)}, bf16[1024,896]{1,0:T(8,128)(2,1)}, u32[]{:S(2)}) copy-start(bf16[1024,896]{1,0:T(8,128)(2,1)} %g_hbm.1) | copy-start | bytes 5505028
  2.1 0.9 %copy-start.1 = (f32[896,32]{0,1:T(8,128)S(1)}, f32[896,32]{0,1:T(8,128)}, u32[]{:S(2)}) copy-start(f32[896,32]{0,1:T(8,128)} %param.7) | copy-start | bytes 344068

commit v2 on v1

--- a/solution.py
+++ b/solution.py
@@ -22,6 +22,8 @@
 P_TILES = 56
 Q_TILES = 28
 SCALE = 1.0 / 32.0
+BAR_AT = 3
+EARLY = 5
 
 NN = (((1,), (0,)), ((), ()))
 NT = (((1,), (1,)), ((), ()))
@@ -65,22 +67,39 @@
     return (work * lax.rsqrt(scale))[:, RANK:2 * RANK]
 
 
-def body(a_hbm, g_hbm, e_hbm, q_ref, c_ref, phat_ref, qloc_ref, nextq_ref,
-         a_buf, g_buf, e_buf, qs, gqs, p_loc, core_buf, p_sum, p_full, p_recv, psplit,
+def far(i):
+    return jnp.where(i < 2, 2 + i, 3 - i)
+
+
+def body(a_hbm, g_hbm, e_hbm, q_hbm, err_ref, phat_ref, nextq_ref,
+         a_buf, g_buf, e_buf, q_buf, c_hi, c_lo, qs, gqs, p_loc, core_buf, p_sum, p_full, p_recv, psplit,
          q_raw, q_recv, q_full,
-         a_sem, g_sem, e_sem, cs_sem, cr_sem, rs_send, rs_recv, ag_send, ag_recv,
+         a_sem, g_sem, e_sem, q_sem, cs_sem, cr_sem, rs_send, rs_recv, ag_send, ag_recv,
          x_send, x_recv, qs_send, qs_recv, qa_send, qa_recv):
     dp = lax.axis_index("dp")
     z = lax.axis_index("tensor")
     core = dp % 2
     plane = dp // 2
+    y = plane // 4
+    x = plane % 4
     chip = plane * 4 + z
     sib = (plane * 2 + 1 - core, z)
 
-    def chip_dev(k):
-        return ((k // 4) * 2 + core, k % 4)
-
+    def chip_at(d):
+        py = (y + far(d // 16)) % 4
+        px = (x + far((d // 4) % 4)) % 4
+        pz = (z + far(d % 4)) % 4
+        return ((py * 4 + px) * 2 + core, pz)
+
+    def dp_at(d):
+        py = (y + far(d // 8)) % 4
+        px = (x + far((d // 2) % 4)) % 4
+        pc = (core + 1 - d % 2) % 2
+        return (py * 4 + px) * 2 + pc
+
+    q_copy = pltpu.make_async_copy(q_hbm, q_buf, q_sem)
     g_copy = pltpu.make_async_copy(g_hbm, g_buf, g_sem)
+    q_copy.start()
     g_copy.start()
     a_copies = []
     e_copies = []
@@ -94,21 +113,16 @@
     bar = pltpu.get_barrier_semaphore()
     pl.semaphore_signal(bar, inc=1, device_id=sib, device_id_type=MESH)
 
-    @pl.loop(0, CHIPS)
-    def _(k):
-        @pl.when(k != chip)
-        def _():
-            pl.semaphore_signal(bar, inc=1, device_id=chip_dev(k), device_id_type=MESH)
-
-    @pl.loop(0, DPS)
-    def _(k):
-        @pl.when(k % 2 != core)
-        def _():
-            @pl.when(k // 2 != plane)
-            def _():
-                pl.semaphore_signal(bar, inc=1, device_id=(k, z), device_id_type=MESH)
-
-    for i, part in enumerate(split3(q_ref[...])):
+    @pl.loop(0, CHIPS - 1)
+    def _(d):
+        pl.semaphore_signal(bar, inc=1, device_id=chip_at(d), device_id_type=MESH)
+
+    @pl.loop(0, DPS // 2 - 1)
+    def _(d):
+        pl.semaphore_signal(bar, inc=1, device_id=(dp_at(2 * d), z), device_id_type=MESH)
+
+    q_copy.wait()
+    for i, part in enumerate(split3(q_buf[...])):
         qs[i * RANK:(i + 1) * RANK, :] = part
     g_copy.wait()
     gq = fold3(mm(qs[...], g_buf[...], NT)) * SCALE
@@ -129,7 +143,8 @@
         core_copy(j).wait_recv()
         p_sum[:, cols] = p_loc[pl.ds(mine, HALF), cols] + core_buf[:, cols]
 
-        def send(i, carry):
+        def send(n, carry):
+            i = (n + chip // 8) % 8
             owner = i * 8 + j
             rows = pl.ds(pl.multiple_of((i // 4) * 8, 8), 8)
             lanes = pl.ds(pl.multiple_of(j * CHUNK + (i % 4) * LANES, LANES), LANES)
@@ -139,7 +154,7 @@
                 pltpu.make_async_remote_copy(
                     src_ref=p_sum.at[rows, lanes], dst_ref=p_recv.at[chip],
                     send_sem=rs_send, recv_sem=rs_recv,
-                    device_id=chip_dev(owner), device_id_type=MESH).start()
+                    device_id=((owner // 4) * 2 + core, owner % 4), device_id_type=MESH).start()
 
             @pl.when(owner == chip)
             def _():
@@ -152,19 +167,26 @@
         a_copies[j].wait()
         e_copies[j].wait()
         p_loc[:, cols] = fold3(mm(gqs[...], a_buf[j]) + mm(qs[...], e_buf[cols, :], NT))
-        if j == 0:
+        if j == BAR_AT:
             pl.semaphore_wait(bar, 1 + (CHIPS - 1) + (DPS // 2 - 1))
-        core_copy(j).start()
-        if j > 0:
-            scatter(j - 1)
+            for i in range(BAR_AT):
+                core_copy(i).start()
+        if j >= BAR_AT:
+            core_copy(j).start()
+        if j > BAR_AT:
+            for i in range(0 if j == BAR_AT + 1 else j - 1, j):
+                scatter(i)
 
     def correct(j):
         cols = pl.ds(j * CHUNK, CHUNK)
-        c_ref[cols, :] = mm(a_buf[j], g_buf[...], TN) * SCALE + e_buf[cols, :].astype(F32)
+        c = mm(a_buf[j], g_buf[...], TN) * SCALE + e_buf[cols, :].astype(F32)
+        hi, lo = split2(c)
+        c_hi[cols, :] = hi
+        c_lo[cols, :] = lo
 
     correct(0)
     scatter(N_CHUNK - 1)
-    for j in range(1, N_CHUNK):
+    for j in range(1, EARLY):
         correct(j)
 
     t_i = chip // 8
@@ -179,15 +201,19 @@
         pltpu.make_async_copy(got, got, rs_recv).wait()
         p_full[t_rows, t_lanes] = jnp.sum(p_recv[...], axis=0)
 
-        def send(k, carry):
-            @pl.when(k != chip)
-            def _():
-                pltpu.make_async_remote_copy(
-                    src_ref=p_full.at[t_rows, t_lanes], dst_ref=p_full.at[t_rows, t_lanes],
-                    send_sem=ag_send, recv_sem=ag_recv,
-                    device_id=chip_dev(k), device_id_type=MESH).start()
+        def send(d, carry):
+            pltpu.make_async_remote_copy(
+                src_ref=p_full.at[t_rows, t_lanes], dst_ref=p_full.at[t_rows, t_lanes],
+                send_sem=ag_send, recv_sem=ag_recv,
+                device_id=chip_at(d), device_id_type=MESH).start()
             return carry
-        lax.fori_loop(0, CHIPS, send, 0)
+        lax.fori_loop(0, CHIPS - 1, send, 0)
+
+    for j in range(EARLY, N_CHUNK):
+        correct(j)
+
+    @pl.when(owns)
+    def _():
         most = p_recv.at[pl.ds(0, P_TILES - 1)]
         pltpu.make_async_copy(most, most, ag_recv).wait()
 
@@ -205,28 +231,24 @@
 
     for i, part in enumerate(split3(p_full[...])):
         psplit[i * RANK:(i + 1) * RANK, :] = part
-    acc = jnp.zeros((RANK, COLS), F32)
-    for j in range(N_CHUNK):
-        cols = pl.ds(j * CHUNK, CHUNK)
-        hi, lo = split2(c_ref[cols, :])
-        acc = acc + fold3(mm(psplit[:, cols], hi) + mm(psplit[:, cols], lo))
-    q_raw[...] = acc
-
-    def q_send(t, carry):
+    acc = jnp.zeros((3 * RANK, COLS), F32)
+    for j in range(N_CHUNK):
+        cols = pl.ds(j * CHUNK, CHUNK)
+        acc = acc + (mm(psplit[:, cols], c_hi[cols, :]) + mm(psplit[:, cols], c_lo[cols, :]))
+    q_raw[...] = fold3(acc)
+
+    def q_send(d, carry):
+        t = dp_at(d)
         rows = pl.ds(pl.multiple_of((t // 7) * 8, 8), 8)
         lanes = pl.ds(pl.multiple_of((t % 7) * LANES, LANES), LANES)
 
-        @pl.when(t != dp)
+        @pl.when(t < Q_TILES)
         def _():
             pltpu.make_async_remote_copy(
                 src_ref=q_raw.at[rows, lanes], dst_ref=q_recv.at[dp],
                 send_sem=qs_send, recv_sem=qs_recv, device_id=(t, z), device_id_type=MESH).start()
-
-        @pl.when(t == dp)
-        def _():
-            q_recv[dp] = q_raw[rows, lanes]
         return carry
-    lax.fori_loop(0, Q_TILES, q_send, 0)
+    lax.fori_loop(0, DPS - 1, q_send, 0)
 
     gram9 = mm(psplit[...], psplit[...], NT)
     gram = jnp.zeros((RANK, RANK), F32)
@@ -234,6 +256,11 @@
         for c in range(3):
             gram = gram + gram9[r * RANK:(r + 1) * RANK, c * RANK:(c + 1) * RANK]
     inv = inverse_factor(gram)
+    inv_parts = split3(inv)
+    inv_left = jnp.concatenate([inv_parts[0], inv_parts[0], inv_parts[1], inv_parts[0], inv_parts[1], inv_parts[2]], axis=1)
+
+    def six(parts):
+        return jnp.concatenate([parts[0], parts[1], parts[0], parts[2], parts[1], parts[0]], axis=0)
 
     q_owns = dp < Q_TILES
     t = jnp.minimum(dp, Q_TILES - 1)
@@ -242,24 +269,17 @@
 
     @pl.when(q_owns)
     def _():
+        q_recv[dp] = q_raw[q_rows, q_lanes]
         got = q_recv.at[pl.ds(0, DPS - 1)]
         pltpu.make_async_copy(got, got, qs_recv).wait()
         q_full[q_rows, q_lanes] = jnp.sum(q_recv[...], axis=0)
 
-        def send(k, carry):
-            @pl.when(k != dp)
-            def _():
-                pltpu.make_async_remote_copy(
-                    src_ref=q_full.at[q_rows, q_lanes], dst_ref=q_full.at[q_rows, q_lanes],
-                    send_sem=qa_send, recv_sem=qa_recv, device_id=(k, z), device_id_type=MESH).start()
+        def send(d, carry):
+            pltpu.make_async_remote_copy(
+                src_ref=q_full.at[q_rows, q_lanes], dst_ref=q_full.at[q_rows, q_lanes],
+                send_sem=qa_send, recv_sem=qa_recv, device_id=(dp_at(d), z), device_id_type=MESH).start()
             return carry
-        lax.fori_loop(0, DPS, send, 0)
-
-    inv_parts = split3(inv)
-    inv_left = jnp.concatenate([inv_parts[0], inv_parts[0], inv_parts[1], inv_parts[0], inv_parts[1], inv_parts[2]], axis=1)
-
-    def six(parts):
-        return jnp.concatenate([parts[0], parts[1], parts[0], parts[2], parts[1], parts[0]], axis=0)
+        lax.fori_loop(0, DPS - 1, send, 0)
 
     p_hat = mm(inv_left, six((psplit[:RANK, :], psplit[RANK:2 * RANK, :], psplit[2 * RANK:, :])))
     ph = jnp.transpose(p_hat)
@@ -268,9 +288,11 @@
     phat_ref[:, RANK:2 * RANK] = ph_hi
     phat_ref[:, 2 * RANK:] = ph_lo
     q_hi, q_lo = split2(mm(inv_left, six(split3(q_raw[...]))))
-    qloc_ref[:RANK, :] = q_hi
-    qloc_ref[RANK:2 * RANK, :] = q_lo
-    qloc_ref[2 * RANK:, :] = q_hi
+    q_right = jnp.concatenate([q_hi, q_lo, q_hi], axis=0)
+    for j in range(N_CHUNK):
+        cols = pl.ds(j * CHUNK, CHUNK)
+        c = c_hi[cols, :].astype(F32) + c_lo[cols, :].astype(F32)
+        err_ref[cols, :] = (c - mm(phat_ref[cols, :], q_right)).astype(BF16)
 
     @pl.when(q_owns)
     def _():
@@ -319,16 +341,18 @@
     return pl.pallas_call(
         body,
         out_shape=(
-            pltpu.VMEM((ROWS, COLS), F32),
+            pltpu.VMEM((ROWS, COLS), BF16),
             pltpu.VMEM((ROWS, 3 * RANK), BF16),
-            pltpu.VMEM((3 * RANK, COLS), BF16),
             pltpu.VMEM((RANK, COLS), F32),
         ),
-        in_specs=[hbm, hbm, hbm, vm],
-        out_specs=(vm, vm, vm, vm),
+        in_specs=[hbm, hbm, hbm, hbm],
+        out_specs=(vm, vm, vm),
         scratch_shapes=[
             pltpu.VMEM((N_CHUNK, TOK, CHUNK), BF16),
             pltpu.VMEM((TOK, COLS), BF16),
+            pltpu.VMEM((ROWS, COLS), BF16),
+            pltpu.VMEM((RANK, COLS), F32),
+            pltpu.VMEM((ROWS, COLS), BF16),
             pltpu.VMEM((ROWS, COLS), BF16),
             pltpu.VMEM((3 * RANK, COLS), BF16),
             pltpu.VMEM((3 * RANK, TOK), BF16),
@@ -341,51 +365,57 @@
             pltpu.VMEM((RANK, COLS), F32),
             pltpu.VMEM((DPS, 8, LANES), F32),
             pltpu.VMEM((RANK, COLS), F32),
-            dma((N_CHUNK,)), dma, dma((N_CHUNK,)), dma((N_CHUNK,)), dma((N_CHUNK,)),
+            dma((N_CHUNK,)), dma, dma((N_CHUNK,)), dma, dma((N_CHUNK,)), dma((N_CHUNK,)),
             dma, dma, dma, dma, dma, dma, dma, dma, dma, dma,
         ],
         compiler_params=pltpu.CompilerParams(
-            collective_id=0, has_side_effects=True, vmem_limit_bytes=36 * 2**20),
+            collective_id=0, has_side_effects=True, vmem_limit_bytes=54 * 2**20),
         name="factors",
     )(a, g, e, q)
 
 
-def out_body(c_ref, phat_ref, qloc_ref, nextq_ref, upd_ref, err_ref, nq_ref, nqs):
-    @pl.when(pl.program_id(0) == 0)
-    def _():
-        hi, lo = split2(nextq_ref[...])
-        nqs[:RANK, :] = hi
-        nqs[RANK:2 * RANK, :] = lo
-        nqs[2 * RANK:, :] = hi
-        nq_ref[...] = nextq_ref[...]
-    rows = pl.ds(pl.multiple_of(pl.program_id(0) * CHUNK, CHUNK), CHUNK)
-    ph = phat_ref[rows, :]
-    err_ref[...] = (c_ref[rows, :] - mm(ph, qloc_ref[...])).astype(BF16)
-    upd_ref[...] = mm(ph, nqs[...]).astype(BF16)
-
-
-def outputs(c, phat, qloc, nextq):
+def out_body(err_vm, phat_ref, nextq_ref, upd_hbm, err_hbm, nq_ref, upd_buf, err_sem, upd_sem):
+    err_copy = pltpu.make_async_copy(err_vm, err_hbm, err_sem)
+    err_copy.start()
+    nq_ref[...] = nextq_ref[...]
+    hi, lo = split2(nextq_ref[...])
+    right = jnp.concatenate([hi, lo, hi], axis=0)
+    copies = []
+    for j in range(N_CHUNK):
+        rows = pl.ds(j * CHUNK, CHUNK)
+        upd_buf[rows, :] = mm(phat_ref[rows, :], right).astype(BF16)
+        copies.append(pltpu.make_async_copy(upd_buf.at[rows, :], upd_hbm.at[rows, :], upd_sem.at[j]))
+        copies[j].start()
+    err_copy.wait()
+    for copy in copies:
+        copy.wait()
+
+
+def outputs(err, phat, nextq):
     vm = pl.BlockSpec(memory_space=pltpu.VMEM)
-    block = pl.BlockSpec((CHUNK, COLS), lambda i: (i, 0))
+    hbm = pl.BlockSpec(memory_space=pltpu.HBM)
     return pl.pallas_call(
         out_body,
-        grid=(N_CHUNK,),
         out_shape=(
             jax.ShapeDtypeStruct((ROWS, COLS), BF16),
             jax.ShapeDtypeStruct((ROWS, COLS), BF16),
             jax.ShapeDtypeStruct((RANK, COLS), F32),
         ),
-        in_specs=[vm, vm, vm, vm],
-        out_specs=(block, block, pl.BlockSpec((RANK, COLS), lambda i: (0, 0))),
-        scratch_shapes=[pltpu.VMEM((3 * RANK, COLS), BF16)],
-        compiler_params=pltpu.CompilerParams(vmem_limit_bytes=24 * 2**20),
+        in_specs=[vm, vm, vm],
+        out_specs=(hbm, hbm, vm),
+        scratch_shapes=[
+            pltpu.VMEM((ROWS, COLS), BF16),
+            pltpu.SemaphoreType.DMA,
+            pltpu.SemaphoreType.DMA((N_CHUNK,)),
+        ],
+        compiler_params=pltpu.CompilerParams(vmem_limit_bytes=40 * 2**20),
         name="outputs",
-    )(c, phat, qloc, nextq)
+    )(err, phat, nextq)
 
 
 def shards(activations, out_grads, error_buffer, basis_q):
-    c, phat, qloc, nextq = factors(activations, out_grads, error_buffer[0], basis_q.T)
-    update, new_error, next_q = outputs(c, phat, qloc, nextq)
+    err, phat, nextq = factors(activations, out_grads, error_buffer[0], basis_q.T)
+    update, new_error, next_q = outputs(err, phat, nextq)
     return update, new_error[None], next_q.T
 
 

time: 55.1 us -> 50.9 us (0.924)
  local copies, waits for them, and re-layouts: 2.39 us -> 0 us
  Pallas kernels: 51.9 us -> 50 us
    unnamed x4 -> x0, local copies, waits for them, and re-layouts: 2.39 us -> none
    pallas_call x2, Pallas kernels: 51.9 us -> 50 us  [the longest x1 44.1 us: factors(): pl.pallas_call(body, out_shape=(pltpu.VMEM((ROWS, COLS), BF16), pltpu.VME...]
where the time goes in v2:
time: 50.9 us; the launch traced here: 50.8 us
  Pallas kernels  50 us (98%)
  between operations  0.8 us (2%)
    pallas_call x1, Pallas kernels, factors(): pl.pallas_call(body, out_shape=(pltpu.VMEM((ROWS, COLS), BF16), pltpu.VME...  44.1 us
    pallas_call x1, Pallas kernels, outputs(): pl.pallas_call(out_body, out_shape=(jax.ShapeDtypeStruct((ROWS, COLS), BF...  5.9 us

profile of v2, /device:TPU:1, one launch (start us, length us, event | category | flops | bytes accessed | tf_op | source)
XLA Modules:
  0.0 50.8 jit_solution(17043746258973274638)
XLA Ops:
  0.6 44.1 %factors.1 = (bf16[3584,896]{1,0:T(8,128)(2,1)S(1)}, bf16[3584,96]{1,0:T(8,128)(2,1)S(1)}, f32[32,896]{1,0:T(8,128)S(1)}) custom-call(bf16[1024,3584]{1,0:T(8,128)(2,1)} %a_hbm.1, bf16[1024,896]{1,0:T(8,128)(2,1)} %g_hbm.1, bf16[3584,896]{1,0:T(8,128)(2,1)} %bitcast.4, f32[32,896]{1,0:T(8,128)} %bitcast.5), custom_call_target="tpu_custom_call" | custom-call | tf_op jit(solution)/shard_map/factors/pallas_call | solution.py:341
  44.7 5.9 %outputs.1 = (bf16[3584,896]{1,0:T(8,128)(2,1)}, bf16[3584,896]{1,0:T(8,128)(2,1)}, f32[32,896]{1,0:T(8,128)}) custom-call(bf16[3584,896]{1,0:T(8,128)(2,1)S(1)} %get-tuple-element.9.err_vm, bf16[3584,96]{1,0:T(8,128)(2,1)S(1)} %get-tuple-element.10.phat_ref, f32[32,896]{1,0:T(8,128)S(1)} %get-tuple-element.11.nextq_ref), custom_call_target="tpu_custom_call" | custom-call | tf_op jit(solution)/shard_map/outputs/pallas_call | solution.py:397

commit v3 on v2

v3 whole, which is shorter than its diff:
```python
import jax
import jax.numpy as jnp
from jax import lax
from jax.experimental import pallas as pl
from jax.experimental.pallas import tpu as pltpu
from jax.sharding import PartitionSpec as P

MESH = pl.DeviceIdType.MESH
F32 = jnp.float32
BF16 = jnp.bfloat16

ROWS = 3584
COLS = 896
TOK = 1024
RANK = 32
HALF = RANK // 2
CHUNK = 512
N_CHUNK = ROWS // CHUNK
CHIPS = 64
DPS = 32
LANES = 128
P_TILES = 56
Q_TILES = 28
SCALE = 1.0 / 32.0
G_PARTS = 4
BAR_AT = 6
EARLY = 4
CUT = 14

NN = (((1,), (0,)), ((), ()))
NT = (((1,), (1,)), ((), ()))
TN = (((0,), (0,)), ((), ()))


def mm(a, b, dims=NN):
    return lax.dot_general(a, b, dims, preferred_element_type=F32)


def split2(x):
    hi = x.astype(BF16)
    lo = (x - hi.astype(F32)).astype(BF16)
    return hi, lo


def split3(x):
    hi = x.astype(BF16)
    rest = x - hi.astype(F32)
    mid = rest.astype(BF16)
    lo = (rest - mid.astype(F32)).astype(BF16)
    return hi, mid, lo


def fold3(x):
    return x[:RANK] + x[RANK:2 * RANK] + x[2 * RANK:]


def eliminate(work, scale, first, last):
    row_id = lax.broadcasted_iota(jnp.int32, (RANK, LANES), 0)
    for j in range(first, last):
        row = work[j:j + 1, :]
        piv = jnp.broadcast_to(work[j:j + 1, j:j + 1], (1, LANES))
        col = jnp.broadcast_to(work[:, j:j + 1], (RANK, LANES))
        scale = jnp.where(row_id == j, piv, scale)
        work = work - jnp.where(row_id > j, col * (row / piv), 0.0)
    return work, scale


def far(i):
    return jnp.where(i < 2, 2 + i, 3 - i)


def body(a_hbm, g_hbm, e_hbm, q_hbm, err_ref, phat_ref, nextq_ref,
         a_buf, g_buf, e_buf, q_buf, c_parts, qs, gqs, p_loc, core_buf, p_sum, p_full, p_recv, psplit,
         q_raw, q_recv, q_full,
         a_sem, g_sem, e_sem, q_sem, cs_sem, cr_sem, rs_send, rs_recv, ag_send, ag_recv,
         x_send, x_recv, qs_send, qs_recv, qa_send, qa_recv):
    dp = lax.axis_index("dp")
    z = lax.axis_index("tensor")
    core = dp % 2
    plane = dp // 2
    y = plane // 4
    x = plane % 4
    chip = plane * 4 + z
    sib = (plane * 2 + 1 - core, z)

    zs = tuple((z + step) % 4 for step in (2, 1, 3, 0))

    def plane_at(o):
        return ((y + far(o // 4)) % 4) * 4 + (x + far(o % 4)) % 4

    q_copy = pltpu.make_async_copy(q_hbm, q_buf, q_sem)
    q_copy.start()
    g_copies = []
    for i in range(G_PARTS):
        toks = pl.ds(i * (TOK // G_PARTS), TOK // G_PARTS)
        g_copies.append(pltpu.make_async_copy(g_hbm.at[toks, :], g_buf.at[toks, :], g_sem.at[i]))
        g_copies[i].start()
    a_copies = []
    e_copies = []
    for j in range(N_CHUNK):
        cols = pl.ds(j * CHUNK, CHUNK)
        a_copies.append(pltpu.make_async_copy(a_hbm.at[:, cols], a_buf.at[j], a_sem.at[j]))
        e_copies.append(pltpu.make_async_copy(e_hbm.at[cols, :], e_buf.at[cols, :], e_sem.at[j]))
    a_copies[0].start()
    e_copies[0].start()

    bar = pltpu.get_barrier_semaphore()

    def greet(there):
        pl.semaphore_signal(bar, inc=1, device_id=there, device_id_type=MESH)

    def greet_planes(first, last):
        def one(o, carry):
            there = plane_at(o) * 2
            for pz in zs:
                greet((there + core, pz))
            greet((there + 1 - core, z))
            return carry
        lax.fori_loop(first, last, one, 0)

    greet_planes(0, 11)

    q_copy.wait()
    for i, part in enumerate(split3(q_buf[...])):
        qs[i * RANK:(i + 1) * RANK, :] = part
    for i in range(G_PARTS):
        g_copies[i].wait()
    for j in range(1, N_CHUNK):
        a_copies[j].start()
        e_copies[j].start()
    greet_planes(11, 15)
    for pz in zs[:3]:
        greet((dp, pz))
    greet(sib)
    gq = fold3(mm(qs[...], g_buf[...], NT)) * SCALE
    for i, part in enumerate(split3(gq)):
        gqs[i * RANK:(i + 1) * RANK, :] = part

    mine = pl.multiple_of(core * HALF, HALF)
    other = pl.multiple_of(HALF - core * HALF, HALF)

    def core_copy(j):
        cols = pl.ds(j * CHUNK, CHUNK)
        return pltpu.make_async_remote_copy(
            src_ref=p_loc.at[pl.ds(other, HALF), cols], dst_ref=core_buf.at[:, cols],
            send_sem=cs_sem.at[j], recv_sem=cr_sem.at[j], device_id=sib, device_id_type=MESH)

    for j in range(N_CHUNK):
        cols = pl.ds(j * CHUNK, CHUNK)
        a_copies[j].wait()
        e_copies[j].wait()
        p_loc[:, cols] = fold3(mm(gqs[...], a_buf[j]) + mm(qs[...], e_buf[cols, :], NT))
        if j == BAR_AT:
            pl.semaphore_wait(bar, (CHIPS - 1) + (DPS // 2 - 1) + 1)
            for i in range(BAR_AT):
                core_copy(i).start()
        if j >= BAR_AT:
            core_copy(j).start()

    def tile(k):
        j = jnp.minimum(k % 8, N_CHUNK - 1)
        i = k // 8
        return pl.multiple_of((i // 4) * 8, 8), pl.ds(pl.multiple_of(j * CHUNK + (i % 4) * LANES, LANES), LANES)

    def scatter(odd, chunks):
        for j in chunks:
            cols = pl.ds(j * CHUNK, CHUNK)
            core_copy(j).wait_recv()
            p_sum[:, cols] = p_loc[pl.ds(mine, HALF), cols] + core_buf[:, cols]

        def send(o, carry):
            place = ((y + far(o // 2)) % 4) * 4 + ((x // 2 + 1 + o) % 2) * 2 + odd
            for pz in zs:
                k = place * 4 + pz
                first, lanes = tile(k)

                @pl.when(jnp.logical_and(k != chip, k % 8 < N_CHUNK))
                def _():
                    pltpu.make_async_remote_copy(
                        src_ref=p_sum.at[pl.ds(first, 8), lanes], dst_ref=p_recv.at[chip],
                        send_sem=rs_send, recv_sem=rs_recv,
                        device_id=(place * 2 + core, pz), device_id_type=MESH).start()
            return carry
        lax.fori_loop(0, 8, send, 0)

    scatter(0, range(4))
    scatter(1, range(4, N_CHUNK))

    def correct(j):
        cols = pl.ds(j * CHUNK, CHUNK)
        c = mm(a_buf[j], g_buf[...], TN) * SCALE + e_buf[cols, :].astype(F32)
        hi, lo = split2(c)
        c_parts[cols, :COLS] = hi
        c_parts[cols, COLS:COLS + LANES] = lo[:, COLS - LANES:]
        c_parts[cols, COLS + LANES:] = lo[:, :COLS - LANES]

    for j in range(EARLY):
        correct(j)

    t_j = chip % 8
    owns = t_j < N_CHUNK
    t_c = jnp.minimum(t_j, N_CHUNK - 1)
    t_first, t_lanes = tile(chip)
    t_rows = pl.ds(pl.multiple_of(core * HALF + t_first, 8), 8)

    @pl.when(owns)
    def _():
        p_recv[chip] = p_sum[pl.ds(t_first, 8), t_lanes]
        got = p_recv.at[pl.ds(0, CHIPS - 1)]
        pltpu.make_async_copy(got, got, rs_recv).wait()
        p_full[t_rows, t_lanes] = jnp.sum(p_recv[...], axis=0)

        def send(there):
            pltpu.make_async_remote_copy(
                src_ref=p_full.at[t_rows, t_lanes], dst_ref=p_full.at[t_rows, t_lanes],
                send_sem=ag_send, recv_sem=ag_recv.at[t_c],
                device_id=there, device_id_type=MESH).start()

        def send_plane(o, carry):
            there = plane_at(o) * 2 + core
            for pz in zs:
                send((there, pz))
            return carry
        lax.fori_loop(0, 15, send_plane, 0)
        for pz in zs[:3]:
            send((dp, pz))

    for j in range(EARLY, N_CHUNK):
        correct(j)

    def swap(j):
        part = p_full.at[pl.ds(mine, HALF), pl.ds(j * CHUNK, CHUNK)]
        return pltpu.make_async_remote_copy(
            src_ref=part, dst_ref=part, send_sem=x_send.at[j], recv_sem=x_recv.at[j],
            device_id=sib, device_id_type=MESH)

    for j in range(N_CHUNK):
        @pl.when(t_j == j)
        def _():
            most = p_recv.at[pl.ds(0, 7)]
            pltpu.make_async_copy(most, most, ag_recv.at[j]).wait()

        @pl.when(t_j != j)
        def _():
            most = p_recv.at[pl.ds(0, 8)]
            pltpu.make_async_copy(most, most, ag_recv.at[j]).wait()
        swap(j).start()
    for j in range(N_CHUNK):
        swap(j).wait_recv()

    for i, part in enumerate(split3(p_full[...])):
        psplit[i * RANK:(i + 1) * RANK, :] = part
    for first, tiles in ((0, 2), (2, 2), (4, 2), (6, 1)):
        cols = pl.ds(first * LANES, tiles * LANES)
        if tiles == 2:
            low = pl.ds(COLS + (first + 1) * LANES, tiles * LANES)
            q_raw[:, cols] = fold3(mm(psplit[...], c_parts[:, cols]) + mm(psplit[...], c_parts[:, low]))
        else:
            both = fold3(mm(psplit[...], c_parts[:, COLS - LANES:COLS + LANES]))
            q_raw[:, cols] = both[:, :LANES] + both[:, LANES:]

        def q_send(n, carry):
            t = first * 4 + (n + plane) % (tiles * 4)
            rows = pl.ds(pl.multiple_of((t % 4) * 8, 8), 8)
            lanes = pl.ds(pl.multiple_of((t // 4) * LANES, LANES), LANES)

            @pl.when(t != dp)
            def _():
                pltpu.make_async_remote_copy(
                    src_ref=q_raw.at[rows, lanes], dst_ref=q_recv.at[dp],
                    send_sem=qs_send, recv_sem=qs_recv, device_id=(t, z), device_id_type=MESH).start()

            @pl.when(t == dp)
            def _():
                q_recv[dp] = q_raw[rows, lanes]
            return carry
        lax.fori_loop(0, tiles * 4, q_send, 0)

    gram9 = mm(psplit[...], psplit[...], NT)
    gram = jnp.zeros((RANK, RANK), F32)
    for r in range(3):
        for c in range(3):
            gram = gram + gram9[r * RANK:(r + 1) * RANK, c * RANK:(c + 1) * RANK]
    row_id = lax.broadcasted_iota(jnp.int32, (RANK, LANES), 0)
    lane_id = lax.broadcasted_iota(jnp.int32, (RANK, LANES), 1)
    work = jnp.concatenate([gram, jnp.zeros((RANK, LANES - RANK), F32)], axis=1)
    work = work + (lane_id == row_id + RANK).astype(F32)
    work, scale = eliminate(work, jnp.zeros((RANK, LANES), F32), 0, CUT)
    q_owns = dp < Q_TILES
    t = jnp.minimum(dp, Q_TILES - 1)
    q_rows = pl.ds(pl.multiple_of((t % 4) * 8, 8), 8)
    q_lanes = pl.ds(pl.multiple_of((t // 4) * LANES, LANES), LANES)

    @pl.when(q_owns)
    def _():
        got = q_recv.at[pl.ds(0, DPS - 1)]
        pltpu.make_async_copy(got, got, qs_recv).wait()
        q_full[q_rows, q_lanes] = jnp.sum(q_recv[...], axis=0)

        def send(there):
            pltpu.make_async_remote_copy(
                src_ref=q_full.at[q_rows, q_lanes], dst_ref=q_full.at[q_rows, q_lanes],
                send_sem=qa_send, recv_sem=qa_recv, device_id=(there, z), device_id_type=MESH).start()

        def send_plane(o, carry):
            there = plane_at(o) * 2
            send(there + core)
            send(there + 1 - core)
            return carry
        lax.fori_loop(0, 15, send_plane, 0)
        send(plane * 2 + 1 - core)

    work, scale = eliminate(work, scale, CUT, RANK)
    inv = (work * lax.rsqrt(scale))[:, RANK:2 * RANK]
    inv_parts = split3(inv)
    inv_left = jnp.concatenate([inv_parts[0], inv_parts[0], inv_parts[1], inv_parts[0], inv_parts[1], inv_parts[2]], axis=1)

    def six(parts):
        return jnp.concatenate([parts[0], parts[1], parts[0], parts[2], parts[1], parts[0]], axis=0)

    p_hat = mm(inv_left, six((psplit[:RANK, :], psplit[RANK:2 * RANK, :], psplit[2 * RANK:, :])))
    ph = jnp.transpose(p_hat)
    ph_hi, ph_lo = split2(ph)
    phat_ref[:, :RANK] = ph_hi
    phat_ref[:, RANK:2 * RANK] = ph_hi
    phat_ref[:, 2 * RANK:] = ph_lo
    q_hi, q_lo = split2(mm(inv_left, six(split3(q_raw[...]))))
    q_right = jnp.concatenate([q_hi, q_lo, q_hi], axis=0)
    for j in range(N_CHUNK):
        cols = pl.ds(j * CHUNK, CHUNK)
        lo = jnp.concatenate([c_parts[cols, COLS + LANES:], c_parts[cols, COLS:COLS + LANES]], axis=1)
        c = c_parts[cols, :COLS].astype(F32) + lo.astype(F32)
        err_ref[cols, :] = (c - mm(phat_ref[cols, :], q_right)).astype(BF16)

    @pl.when(q_owns)
    def _():
        most = q_recv.at[pl.ds(0, Q_TILES - 1)]
        pltpu.make_async_copy(most, most, qa_recv).wait()

    @pl.when(jnp.logical_not(q_owns))
    def _():
        most = q_recv.at[pl.ds(0, Q_TILES)]
        pltpu.make_async_copy(most, most, qa_recv).wait()

    nextq_ref[...] = mm(inv_left, six(split3(q_full[...]))) * (1.0 / DPS)

    for j in range(N_CHUNK):
        core_copy(j).wait_send()
        swap(j).wait_send()

    @pl.when(owns)
    def _():
        sent = p_recv.at[pl.ds(0, P_TILES - 1)]
        pltpu.make_async_copy(sent, sent, rs_send).wait()
        sent = p_recv.at[pl.ds(0, CHIPS - 1)]
        pltpu.make_async_copy(sent, sent, ag_send).wait()

    @pl.when(jnp.logical_not(owns))
    def _():
        sent = p_recv.at[pl.ds(0, P_TILES)]
        pltpu.make_async_copy(sent, sent, rs_send).wait()

    @pl.when(q_owns)
    def _():
        sent = q_recv.at[pl.ds(0, Q_TILES - 1)]
        pltpu.make_async_copy(sent, sent, qs_send).wait()
        sent = q_recv.at[pl.ds(0, DPS - 1)]
        pltpu.make_async_copy(sent, sent, qa_send).wait()

    @pl.when(jnp.logical_not(q_owns))
    def _():
        sent = q_recv.at[pl.ds(0, Q_TILES)]
        pltpu.make_async_copy(sent, sent, qs_send).wait()


def factors(a, g, e, q):
    vm = pl.BlockSpec(memory_space=pltpu.VMEM)
    hbm = pl.BlockSpec(memory_space=pltpu.HBM)
    dma = pltpu.SemaphoreType.DMA
    return pl.pallas_call(
        body,
        out_shape=(
            pltpu.VMEM((ROWS, COLS), BF16),
            pltpu.VMEM((ROWS, 3 * RANK), BF16),
            pltpu.VMEM((RANK, COLS), F32),
        ),
        in_specs=[hbm, hbm, hbm, hbm],
        out_specs=(vm, vm, vm),
        scratch_shapes=[
            pltpu.VMEM((N_CHUNK, TOK, CHUNK), BF16),
            pltpu.VMEM((TOK, COLS), BF16),
            pltpu.VMEM((ROWS, COLS), BF16),
            pltpu.VMEM((RANK, COLS), F32),
            pltpu.VMEM((ROWS, 2 * COLS), BF16),
            pltpu.VMEM((3 * RANK, COLS), BF16),
            pltpu.VMEM((3 * RANK, TOK), BF16),
            pltpu.VMEM((RANK, ROWS), F32),
            pltpu.VMEM((HALF, ROWS), F32),
            pltpu.VMEM((HALF, ROWS), F32),
            pltpu.VMEM((RANK, ROWS), F32),
            pltpu.VMEM((CHIPS, 8, LANES), F32),
            pltpu.VMEM((3 * RANK, ROWS), BF16),
            pltpu.VMEM((RANK, COLS), F32),
            pltpu.VMEM((DPS, 8, LANES), F32),
            pltpu.VMEM((RANK, COLS), F32),
            dma((N_CHUNK,)), dma((G_PARTS,)), dma((N_CHUNK,)), dma, dma((N_CHUNK,)), dma((N_CHUNK,)),
            dma, dma, dma, dma((N_CHUNK,)), dma((N_CHUNK,)), dma((N_CHUNK,)), dma, dma, dma, dma,
        ],
        compiler_params=pltpu.CompilerParams(
            collective_id=0, has_side_effects=True, vmem_limit_bytes=54 * 2**20),
        name="factors",
    )(a, g, e, q)


def out_body(err_vm, phat_ref, nextq_ref, upd_hbm, err_hbm, nq_ref, upd_buf, err_sem, upd_sem):
    err_copy = pltpu.make_async_copy(err_vm, err_hbm, err_sem)
    err_copy.start()
    nq_ref[...] = nextq_ref[...]
    hi, lo = split2(nextq_ref[...])
    right = jnp.concatenate([hi, lo, hi], axis=0)
    copies = []
    for j in range(N_CHUNK):
        rows = pl.ds(j * CHUNK, CHUNK)
        upd_buf[rows, :] = mm(phat_ref[rows, :], right).astype(BF16)
        copies.append(pltpu.make_async_copy(upd_buf.at[rows, :], upd_hbm.at[rows, :], upd_sem.at[j]))
        copies[j].start()
    err_copy.wait()
    for copy in copies:
        copy.wait()


def outputs(err, phat, nextq):
    vm = pl.BlockSpec(memory_space=pltpu.VMEM)
    hbm = pl.BlockSpec(memory_space=pltpu.HBM)
    return pl.pallas_call(
        out_body,
        out_shape=(
            jax.ShapeDtypeStruct((ROWS, COLS), BF16),
            jax.ShapeDtypeStruct((ROWS, COLS), BF16),
            jax.ShapeDtypeStruct((RANK, COLS), F32),
        ),
        in_specs=[vm, vm, vm],
        out_specs=(hbm, hbm, vm),
        scratch_shapes=[
            pltpu.VMEM((ROWS, COLS), BF16),
            pltpu.SemaphoreType.DMA,
            pltpu.SemaphoreType.DMA((N_CHUNK,)),
        ],
        compiler_params=pltpu.CompilerParams(vmem_limit_bytes=40 * 2**20),
        name="outputs",
    )(err, phat, nextq)


def shards(activations, out_grads, error_buffer, basis_q):
    err, phat, nextq = factors(activations, out_grads, error_buffer[0], basis_q.T)
    update, new_error, next_q = outputs(err, phat, nextq)
    return update, new_error[None], next_q.T


def solution(mesh):
    in_specs = (P("dp", None), P("dp", "tensor"), P("dp", None, "tensor"), P("tensor", None))
    out_specs = (P(None, "tensor"), P("dp", None, "tensor"), P("tensor", None))
    return jax.shard_map(shards, mesh=mesh, in_specs=in_specs, out_specs=out_specs, check_vma=False)
```

time: 50.9 us -> 48.4 us (0.951)
  Pallas kernels: 50 us -> 47.5 us
    pallas_call x1, Pallas kernels: 44.1 us -> 41.6 us  [factors(): pl.pallas_call(body, out_shape=(pltpu.VMEM((ROWS, COLS), BF16), pltpu.VME...]
where the time goes in v3:
time: 48.4 us; the launch traced here: 48.3 us
  Pallas kernels  47.5 us (98%)
  between operations  0.8 us (2%)
    pallas_call x1, Pallas kernels, factors(): pl.pallas_call(body, out_shape=(pltpu.VMEM((ROWS, COLS), BF16), pltpu.VME...  41.6 us
    pallas_call x1, Pallas kernels, outputs(): pl.pallas_call(out_body, out_shape=(jax.ShapeDtypeStruct((ROWS, COLS), BF...  5.89 us

profile of v3, /device:TPU:1, one launch (start us, length us, event | category | flops | bytes accessed | tf_op | source)
XLA Modules:
  0.0 48.3 jit_solution(18221160450314646116)
XLA Ops:
  0.6 41.6 %factors.1 = (bf16[3584,896]{1,0:T(8,128)(2,1)S(1)}, bf16[3584,96]{1,0:T(8,128)(2,1)S(1)}, f32[32,896]{1,0:T(8,128)S(1)}) custom-call(bf16[1024,3584]{1,0:T(8,128)(2,1)} %a_hbm.1, bf16[1024,896]{1,0:T(8,128)(2,1)} %g_hbm.1, bf16[3584,896]{1,0:T(8,128)(2,1)} %bitcast.4, f32[32,896]{1,0:T(8,128)} %bitcast.5), custom_call_target="tpu_custom_call" | custom-call | tf_op jit(solution)/shard_map/factors/pallas_call | solution.py:380
  42.3 5.9 %outputs.1 = (bf16[3584,896]{1,0:T(8,128)(2,1)}, bf16[3584,896]{1,0:T(8,128)(2,1)}, f32[32,896]{1,0:T(8,128)}) custom-call(bf16[3584,896]{1,0:T(8,128)(2,1)S(1)} %get-tuple-element.9.err_vm, bf16[3584,96]{1,0:T(8,128)(2,1)S(1)} %get-tuple-element.10.phat_ref, f32[32,896]{1,0:T(8,128)S(1)} %get-tuple-element.11.nextq_ref), custom_call_target="tpu_custom_call" | custom-call | tf_op jit(solution)/shard_map/outputs/pallas_call | solution.py:435

commit v4 on v3

--- a/solution.py
+++ b/solution.py
@@ -23,9 +23,11 @@
 Q_TILES = 28
 SCALE = 1.0 / 32.0
 G_PARTS = 4
-BAR_AT = 6
+BAR_AT = 4
 EARLY = 4
 CUT = 14
+ERR_CUTS = 14
+UPD_CUTS = 28
 
 NN = (((1,), (0,)), ((), ()))
 NT = (((1,), (1,)), ((), ()))
@@ -245,19 +247,28 @@
             most = p_recv.at[pl.ds(0, 8)]
             pltpu.make_async_copy(most, most, ag_recv.at[j]).wait()
         swap(j).start()
-    for j in range(N_CHUNK):
-        swap(j).wait_recv()
-
-    for i, part in enumerate(split3(p_full[...])):
-        psplit[i * RANK:(i + 1) * RANK, :] = part
-    for first, tiles in ((0, 2), (2, 2), (4, 2), (6, 1)):
-        cols = pl.ds(first * LANES, tiles * LANES)
+    def take(first, last):
+        for j in range(first, last):
+            swap(j).wait_recv()
+        cols = pl.ds(first * CHUNK, (last - first) * CHUNK)
+        for i, part in enumerate(split3(p_full[:, cols])):
+            psplit[i * RANK:(i + 1) * RANK, cols] = part
+
+    def product(rows, first, tiles):
         if tiles == 2:
+            high = pl.ds(first * LANES, tiles * LANES)
             low = pl.ds(COLS + (first + 1) * LANES, tiles * LANES)
-            q_raw[:, cols] = fold3(mm(psplit[...], c_parts[:, cols]) + mm(psplit[...], c_parts[:, low]))
-        else:
-            both = fold3(mm(psplit[...], c_parts[:, COLS - LANES:COLS + LANES]))
-            q_raw[:, cols] = both[:, :LANES] + both[:, LANES:]
+            return fold3(mm(psplit[:, rows], c_parts[rows, high]) + mm(psplit[:, rows], c_parts[rows, low]))
+        both = fold3(mm(psplit[:, rows], c_parts[rows, COLS - LANES:COLS + LANES]))
+        return both[:, :LANES] + both[:, LANES:]
+
+    strips = ((0, 2), (2, 2), (4, 2), (6, 1))
+    take(0, 4)
+    for first, tiles in strips:
+        q_raw[:, pl.ds(first * LANES, tiles * LANES)] = product(pl.ds(0, 4 * CHUNK), first, tiles)
+    take(4, N_CHUNK)
+    for first, tiles in strips:
+        q_raw[:, pl.ds(first * LANES, tiles * LANES)] += product(pl.ds(4 * CHUNK, 3 * CHUNK), first, tiles)
 
         def q_send(n, carry):
             t = first * 4 + (n + plane) % (tiles * 4)
@@ -413,18 +424,21 @@
 
 
 def out_body(err_vm, phat_ref, nextq_ref, upd_hbm, err_hbm, nq_ref, upd_buf, err_sem, upd_sem):
-    err_copy = pltpu.make_async_copy(err_vm, err_hbm, err_sem)
-    err_copy.start()
+    copies = []
+
+    def leave(src, dst, rows, sem):
+        copies.append(pltpu.make_async_copy(src.at[rows, :], dst.at[rows, :], sem))
+        copies[-1].start()
+
+    for j in range(ERR_CUTS):
+        leave(err_vm, err_hbm, pl.ds(j * (ROWS // ERR_CUTS), ROWS // ERR_CUTS), err_sem.at[j])
     nq_ref[...] = nextq_ref[...]
     hi, lo = split2(nextq_ref[...])
     right = jnp.concatenate([hi, lo, hi], axis=0)
-    copies = []
-    for j in range(N_CHUNK):
-        rows = pl.ds(j * CHUNK, CHUNK)
+    for j in range(UPD_CUTS):
+        rows = pl.ds(j * (ROWS // UPD_CUTS), ROWS // UPD_CUTS)
         upd_buf[rows, :] = mm(phat_ref[rows, :], right).astype(BF16)
-        copies.append(pltpu.make_async_copy(upd_buf.at[rows, :], upd_hbm.at[rows, :], upd_sem.at[j]))
-        copies[j].start()
-    err_copy.wait()
+        leave(upd_buf, upd_hbm, rows, upd_sem.at[j])
     for copy in copies:
         copy.wait()
 
@@ -443,8 +457,8 @@
         out_specs=(hbm, hbm, vm),
         scratch_shapes=[
             pltpu.VMEM((ROWS, COLS), BF16),
-            pltpu.SemaphoreType.DMA,
-            pltpu.SemaphoreType.DMA((N_CHUNK,)),
+            pltpu.SemaphoreType.DMA((ERR_CUTS,)),
+            pltpu.SemaphoreType.DMA((UPD_CUTS,)),
         ],
         compiler_params=pltpu.CompilerParams(vmem_limit_bytes=40 * 2**20),
         name="outputs",

time: 48.4 us -> 46.8 us (0.967)
  Pallas kernels: 47.5 us -> 45.9 us
    pallas_call x1, Pallas kernels: 41.6 us -> 40 us  [factors(): pl.pallas_call(body, out_shape=(pltpu.VMEM((ROWS, COLS), BF16), pltpu.VME...]
where the time goes in v4:
time: 46.8 us; the launch traced here: 46.7 us
  Pallas kernels  45.9 us (98%)
  between operations  0.8 us (2%)
    pallas_call x1, Pallas kernels, factors(): pl.pallas_call(body, out_shape=(pltpu.VMEM((ROWS, COLS), BF16), pltpu.VME...  40 us
    pallas_call x1, Pallas kernels, outputs(): pl.pallas_call(out_body, out_shape=(jax.ShapeDtypeStruct((ROWS, COLS), BF...  5.84 us

profile of v4, /device:TPU:1, one launch (start us, length us, event | category | flops | bytes accessed | tf_op | source)
XLA Modules:
  0.0 46.7 jit_solution(5577203698133851458)
XLA Ops:
  0.6 40.0 %factors.1 = (bf16[3584,896]{1,0:T(8,128)(2,1)S(1)}, bf16[3584,96]{1,0:T(8,128)(2,1)S(1)}, f32[32,896]{1,0:T(8,128)S(1)}) custom-call(bf16[1024,3584]{1,0:T(8,128)(2,1)} %a_hbm.1, bf16[1024,896]{1,0:T(8,128)(2,1)} %g_hbm.1, bf16[3584,896]{1,0:T(8,128)(2,1)} %bitcast.4, f32[32,896]{1,0:T(8,128)} %bitcast.5), custom_call_target="tpu_custom_call" | custom-call | tf_op jit(solution)/shard_map/factors/pallas_call | solution.py:391
  40.7 5.8 %outputs.1 = (bf16[3584,896]{1,0:T(8,128)(2,1)}, bf16[3584,896]{1,0:T(8,128)(2,1)}, f32[32,896]{1,0:T(8,128)}) custom-call(bf16[3584,896]{1,0:T(8,128)(2,1)S(1)} %get-tuple-element.9.err_vm, bf16[3584,96]{1,0:T(8,128)(2,1)S(1)} %get-tuple-element.10.phat_ref, f32[32,896]{1,0:T(8,128)S(1)} %get-tuple-element.11.nextq_ref), custom_call_target="tpu_custom_call" | custom-call | tf_op jit(solution)/shard_map/outputs/pallas_call | solution.py:449

commit v5 on v4

--- a/solution.py
+++ b/solution.py
@@ -24,7 +24,7 @@
 SCALE = 1.0 / 32.0
 G_PARTS = 4
 BAR_AT = 4
-EARLY = 4
+EARLY = 3
 CUT = 14
 ERR_CUTS = 14
 UPD_CUTS = 28
@@ -423,7 +423,7 @@
     )(a, g, e, q)
 
 
-def out_body(err_vm, phat_ref, nextq_ref, upd_hbm, err_hbm, nq_ref, upd_buf, err_sem, upd_sem):
+def out_body(err_vm, phat_ref, nextq_ref, upd_hbm, err_hbm, nq_hbm, upd_buf, err_sem, upd_sem, nq_sem):
     copies = []
 
     def leave(src, dst, rows, sem):
@@ -432,7 +432,8 @@
 
     for j in range(ERR_CUTS):
         leave(err_vm, err_hbm, pl.ds(j * (ROWS // ERR_CUTS), ROWS // ERR_CUTS), err_sem.at[j])
-    nq_ref[...] = nextq_ref[...]
+    copies.append(pltpu.make_async_copy(nextq_ref, nq_hbm, nq_sem))
+    copies[-1].start()
     hi, lo = split2(nextq_ref[...])
     right = jnp.concatenate([hi, lo, hi], axis=0)
     for j in range(UPD_CUTS):
@@ -454,11 +455,12 @@
             jax.ShapeDtypeStruct((RANK, COLS), F32),
         ),
         in_specs=[vm, vm, vm],
-        out_specs=(hbm, hbm, vm),
+        out_specs=(hbm, hbm, hbm),
         scratch_shapes=[
             pltpu.VMEM((ROWS, COLS), BF16),
             pltpu.SemaphoreType.DMA((ERR_CUTS,)),
             pltpu.SemaphoreType.DMA((UPD_CUTS,)),
+            pltpu.SemaphoreType.DMA,
         ],
         compiler_params=pltpu.CompilerParams(vmem_limit_bytes=40 * 2**20),
         name="outputs",

time: 46.8 us -> 45.9 us (0.981)
  Pallas kernels: 45.9 us -> 45 us
    pallas_call x1, Pallas kernels: 5.84 us -> 5.24 us  [outputs(): pl.pallas_call(out_body, out_shape=(jax.ShapeDtypeStruct((ROWS, COLS), BF...]
where the time goes in v5:
time: 45.9 us; the launch traced here: 45.8 us
  Pallas kernels  45 us (98%)
  between operations  0.8 us (2%)
    pallas_call x1, Pallas kernels, factors(): pl.pallas_call(body, out_shape=(pltpu.VMEM((ROWS, COLS), BF16), pltpu.VME...  39.8 us
    pallas_call x1, Pallas kernels, outputs(): pl.pallas_call(out_body, out_shape=(jax.ShapeDtypeStruct((ROWS, COLS), BF...  5.24 us

profile of v5, /device:TPU:1, one launch (start us, length us, event | category | flops | bytes accessed | tf_op | source)
XLA Modules:
  0.0 45.8 jit_solution(9387529207663110044)
XLA Ops:
  0.6 39.8 %factors.1 = (bf16[3584,896]{1,0:T(8,128)(2,1)S(1)}, bf16[3584,96]{1,0:T(8,128)(2,1)S(1)}, f32[32,896]{1,0:T(8,128)S(1)}) custom-call(bf16[1024,3584]{1,0:T(8,128)(2,1)} %a_hbm.1, bf16[1024,896]{1,0:T(8,128)(2,1)} %g_hbm.1, bf16[3584,896]{1,0:T(8,128)(2,1)} %bitcast.4, f32[32,896]{1,0:T(8,128)} %bitcast.5), custom_call_target="tpu_custom_call" | custom-call | tf_op jit(solution)/shard_map/factors/pallas_call | solution.py:391
  40.4 5.2 %outputs.1 = (bf16[3584,896]{1,0:T(8,128)(2,1)}, bf16[3584,896]{1,0:T(8,128)(2,1)}, f32[32,896]{1,0:T(8,128)}) custom-call(bf16[3584,896]{1,0:T(8,128)(2,1)S(1)} %get-tuple-element.9.err_vm, bf16[3584,96]{1,0:T(8,128)(2,1)S(1)} %get-tuple-element.10.phat_ref, f32[32,896]{1,0:T(8,128)S(1)} %get-tuple-element.11.nextq_ref), custom_call_target="tpu_custom_call" | custom-call | tf_op jit(solution)/shard_map/outputs/pallas_call | solution.py:450
